TPU v7x, 32 devices: a whole 2x2x4 slice. The times are simulated.
32 devices in a mesh: grp: 4 (over y, core), blk: 8 (over z, x).
Axes of the slice: x: 2, y: 2, z: 4, core: 2. Of those that a mesh axis runs over, the one named last changes fastest.
Arguments:
- images: float32 [12288, 1152], P(('grp', 'blk')), may hold values from -6 to 6
- texts: float32 [12288, 1152], P(('grp', 'blk')), may hold values from -6 to 6
- pair_index: int32 [32, 384], P(('grp', 'blk')), may hold values from 0 to 383, each once within a row
Outputs:
- row_loss: float32 [12288], P(('grp', 'blk'))
- image_grad: float32 [12288, 1152], P(('grp', 'blk'))
- text_grad: float32 [12288, 1152], P(('grp', 'blk'))
Inputs may be any that keep to these rules, and one draw needn't show every extreme that they name: Each row of pair_index is a permutation of 0 to 383.
All inputs are finite; a program needn't handle non-finite values.
Results may differ from a plain program's by a relative error of at most 0.0001.
Values sent between devices are 32-bit elements; how exact they have to be, the bound alone decides.
A program may use at most 64 MiB of HBM per device.

v0:
```python
import functools

import jax
import jax.numpy as jnp
from jax import lax
from jax.experimental import pallas as pl
from jax.experimental.pallas import tpu as pltpu
from jax.sharding import PartitionSpec as P

MESH = pl.DeviceIdType.MESH
CHUNK = 128
PIECE = 64
PARTS = CHUNK // PIECE

GROUP, FAR, NEAR = 0, 1, 2


def split(value):
    high = value.astype(jnp.bfloat16)
    return high, (value - high.astype(jnp.float32)).astype(jnp.bfloat16)


def across(left, right):
    return lax.dot_general(left, right, (((1,), (1,)), ((), ())), preferred_element_type=jnp.float32)


def kernel(
    n_grp, n_blk, scale,
    img, txt, pair, loss_out, img_out, txt_out,
    land, own, high, low, acc, match, total,
    own_sem, out_sem, send_sem, relay_sem, recv_sem,
):
    rows, width = img.shape
    pieces = rows // PIECE
    chunks = rows // CHUNK
    g, i = lax.axis_index("grp"), lax.axis_index("blk")
    odd = lax.rem(i, 2)
    relayed = 1 - odd
    partner = (g, i + 1 - 2 * odd)
    ahead, behind = (g, lax.rem(i + 2, n_blk)), (g, lax.rem(i + n_blk - 2, n_blk))
    upper, lower = (lax.rem(g + 1, n_grp), i), (lax.rem(g + n_grp - 1, n_grp), i)

    loads = [
        pltpu.make_async_copy(img, own.at[0], own_sem.at[0]),
        pltpu.make_async_copy(txt, own.at[1], own_sem.at[1]),
    ]
    for load in loads:
        load.start()

    barrier = pltpu.get_barrier_semaphore()
    for device in (partner, ahead, behind, upper, lower):
        pl.semaphore_signal(barrier, inc=1, device_id=device, device_id_type=MESH)
    pl.semaphore_wait(barrier, 5)

    def span(q):
        return pl.ds(pl.multiple_of(q * PIECE, PIECE), PIECE)

    def send(src, slot, q, lane, device):
        return pltpu.make_async_remote_copy(
            src_ref=src.at[span(q)],
            dst_ref=land.at[slot, span(q)],
            send_sem=send_sem.at[lane, q],
            recv_sem=recv_sem.at[slot, q],
            device_id=device,
            device_id_type=MESH,
        )

    def relay(q):
        return pltpu.make_async_remote_copy(
            src_ref=land.at[2 * FAR + relayed, span(q)],
            dst_ref=land.at[2 * NEAR + relayed, span(q)],
            send_sem=relay_sem.at[q],
            recv_sem=recv_sem.at[2 * NEAR + relayed, q],
            device_id=partner,
            device_id_type=MESH,
        )

    def arrived(slot, q):
        pltpu.make_async_remote_copy(
            src_ref=land.at[slot, span(q)],
            dst_ref=land.at[slot, span(q)],
            send_sem=relay_sem.at[q],
            recv_sem=recv_sem.at[slot, q],
            device_id=partner,
            device_id_type=MESH,
        ).wait_recv()

    def send_all(q, _):
        send(txt, 2 * FAR, q, 0, ahead).start()
        send(img, 2 * FAR + 1, q, 1, behind).start()

        @pl.when(odd == 0)
        def _():
            send(txt, 2 * NEAR, q, 2, partner).start()

        @pl.when(odd == 1)
        def _():
            send(img, 2 * NEAR + 1, q, 2, partner).start()

        send(txt, 2 * GROUP, q, 3, lower).start()
        send(img, 2 * GROUP + 1, q, 4, upper).start()
        return 0

    lax.fori_loop(0, pieces, send_all, 0)

    for load in loads:
        load.wait()
    for kind in range(2):
        for c in range(chunks):
            at = pl.ds(c * CHUNK, CHUNK)
            high[kind, at], low[kind, at] = split(own[kind, at])
    index = pair[...]
    by_row = jnp.transpose(
        jnp.broadcast_to(index.astype(jnp.float32), (CHUNK, rows))
    )
    lane = lax.broadcasted_iota(jnp.int32, (rows, CHUNK), 1).astype(jnp.float32)
    row = lax.broadcasted_iota(jnp.int32, (rows, CHUNK), 0)
    for c in range(chunks):
        match[0, c] = (by_row == lane + float(c * CHUNK)).astype(jnp.float32)
        match[1, c] = (row == index[:, c * CHUNK : (c + 1) * CHUNK]).astype(jnp.float32)
    acc[...] = jnp.zeros_like(acc)
    total[...] = jnp.zeros_like(total)

    def meet(kind, their_high, their_low, positive):
        both = across(high[kind], jnp.concatenate([their_high, their_low], axis=0))
        dots = both[:, :CHUNK] + both[:, CHUNK:] + across(low[kind], their_high)
        s = scale * dots - 3.0
        e = jnp.exp(-jnp.abs(s))
        weight = jnp.where(s >= 0.0, 1.0, e) / (1.0 + e)
        if positive is not None:
            weight = weight - positive
        if kind == 0:
            loss = jnp.maximum(s, 0.0) + jnp.log1p(e)
            if positive is not None:
                loss = loss - positive * s
            total[...] += loss
        w_high, w_low = split(scale * weight)
        w_both = jnp.concatenate([w_high, w_low], axis=1)
        for t in range(0, width, 384):
            cut = slice(t, min(t + 384, width))
            top = their_high[:, cut]
            acc[kind, :, cut] += jnp.dot(
                w_both, jnp.concatenate([top, top], axis=0), preferred_element_type=jnp.float32
            ) + jnp.dot(w_high, their_low[:, cut], preferred_element_type=jnp.float32)

    def own_step(c, _):
        at = pl.ds(pl.multiple_of(c * CHUNK, CHUNK), CHUNK)
        for kind in range(2):
            meet(kind, high[1 - kind, at], low[1 - kind, at], match[kind, c])
        return 0

    lax.fori_loop(0, chunks, own_step, 0)

    def step(n, _):
        c, m = n // 3, n % 3
        for h in range(PARTS):
            q = c * PARTS + h
            arrived(2 * m + relayed, q)

            @pl.when(m == FAR)
            def _():
                relay(q).start()

        for h in range(PARTS):
            arrived(2 * m + odd, c * PARTS + h)
        at = pl.ds(pl.multiple_of(c * CHUNK, CHUNK), CHUNK)
        for kind in range(2):
            meet(kind, *split(land[2 * m + kind, at]), None)
        return 0

    lax.fori_loop(0, 3 * chunks, step, 0)

    stores = [
        pltpu.make_async_copy(acc.at[0], img_out, out_sem.at[0]),
        pltpu.make_async_copy(acc.at[1], txt_out, out_sem.at[1]),
    ]
    for store in stores:
        store.start()
    loss_out[...] = jnp.sum(jnp.transpose(total[...]), axis=0, keepdims=True) / (4.0 * rows)

    def drain(q, _):
        for line, device in enumerate((ahead, behind, partner, lower, upper)):
            send(txt, 0, q, line, device).wait_send()
        relay(q).wait_send()
        return 0

    lax.fori_loop(0, pieces, drain, 0)
    for store in stores:
        store.wait()


def on_device(n_grp, n_blk, images, texts, pair_index):
    rows, width = images.shape
    scale = 2.0 * width ** (-0.5)
    pieces = rows // PIECE
    any_space = pl.BlockSpec(memory_space=pl.ANY)
    vmem = pl.BlockSpec(memory_space=pltpu.VMEM)
    block = jax.ShapeDtypeStruct((rows, width), jnp.float32)
    loss, image_grad, text_grad = pl.pallas_call(
        functools.partial(kernel, n_grp, n_blk, scale),
        out_shape=(jax.ShapeDtypeStruct((1, rows), jnp.float32), block, block),
        in_specs=[any_space, any_space, vmem],
        out_specs=(vmem, any_space, any_space),
        scratch_shapes=[
            pltpu.VMEM((6, rows, width), jnp.float32),
            pltpu.VMEM((2, rows, width), jnp.float32),
            pltpu.VMEM((2, rows, width), jnp.bfloat16),
            pltpu.VMEM((2, rows, width), jnp.bfloat16),
            pltpu.VMEM((2, rows, width), jnp.float32),
            pltpu.VMEM((2, rows // CHUNK, rows, CHUNK), jnp.float32),
            pltpu.VMEM((rows, CHUNK), jnp.float32),
            pltpu.SemaphoreType.DMA((2,)),
            pltpu.SemaphoreType.DMA((2,)),
            pltpu.SemaphoreType.DMA((5, pieces)),
            pltpu.SemaphoreType.DMA((pieces,)),
            pltpu.SemaphoreType.DMA((6, pieces)),
        ],
        compiler_params=pltpu.CompilerParams(
            collective_id=0, has_side_effects=True, vmem_limit_bytes=52 * 1024 * 1024
        ),
        cost_estimate=pl.CostEstimate(
            flops=16 * 3 * 2 * rows * rows * width,
            bytes_accessed=4 * 4 * rows * width,
            transcendentals=8 * rows * rows,
        ),
    )(images, texts, pair_index)
    return loss.reshape(rows), image_grad, text_grad


def solution(mesh):
    n_grp, n_blk = mesh.shape["grp"], mesh.shape["blk"]
    assert n_blk % 2 == 0
    in_specs = (P(("grp", "blk"), None), P(("grp", "blk"), None), P(("grp", "blk"), None))
    out_specs = (P(("grp", "blk")), P(("grp", "blk"), None), P(("grp", "blk"), None))
    return jax.shard_map(
        functools.partial(on_device, n_grp, n_blk),
        mesh=mesh, in_specs=in_specs, out_specs=out_specs, check_vma=False,
    )
```

profile of v0, /device:TPU:0, one launch (start us, length us, event | category | flops | bytes accessed | tf_op | source)
XLA Modules:
  0.0 104.4 jit_solution(16948538159343372324)
XLA Ops:
  0.6 0.0 copy-start
  0.6 0.7 copy-done
  1.3 99.2 %shard_map.58 = (f32[1,384]{1,0:T(1,128)S(1)}, f32[384,1152]{1,0:T(8,128)S(1)}, f32[384,1152]{1,0:T(8,128)}) custom-call(f32[384,1152]{1,0:T(8,128)} %img.1, f32[384,1152]{1,0:T(8,128)} %txt.1, s32[1,384]{1,0:T(1,128)S(1)} %copy-done), custom_call_target="tpu_custom_call" | custom-call | flops 16307453952 | bytes 7077888 | tf_op jit(solution)/shard_map/pallas_call | solution.py:199
  100.5 0.6 reduce
  101.1 0.0 copy-start.1
  101.1 1.2 %copy.8 = f32[384,1152]{1,0:T(8,128)} copy(f32[384,1152]{1,0:T(8,128)S(1)} %get-tuple-element.13) | data formatting | bytes 3538944
  102.3 0.9 copy-done.1
  103.2 1.2 %copy.9 = f32[384,1152]{1,0:T(8,128)} copy(f32[384,1152]{1,0:T(8,128)S(1)} %copy-done.1) | data formatting | bytes 3538944
Async XLA Ops:
  0.6 0.7 copy-start
  101.1 2.1 %copy-start.1 = (f32[384,1152]{1,0:T(8,128)S(1)}, f32[384,1152]{1,0:T(8,128)}, u32[]{:S(2)}) copy-start(f32[384,1152]{1,0:T(8,128)} %get-tuple-element.14) | copy-start | bytes 5308420
where the time goes:
time: 105 us; the launch traced here: 104 us
  Pallas kernels  99.2 us (94%)
  local copies, waits for them, and re-layouts  3.99 us (4%)
    pallas_call x1, Pallas kernels, on_device(): pl.pallas_call(functools.partial(kernel, n_grp, n_blk, scale), out_shape=...  99.2 us
    unnamed x6, local copies, waits for them, and re-layouts  3.99 us

commit v1 on v0

--- a/solution.py
+++ b/solution.py
@@ -85,23 +85,34 @@
             device_id_type=MESH,
         ).wait_recv()
 
-    def send_all(q, _):
-        send(txt, 2 * FAR, q, 0, ahead).start()
-        send(img, 2 * FAR + 1, q, 1, behind).start()
-
+    def send_first(q, _):
         @pl.when(odd == 0)
         def _():
+            send(img, 2 * FAR + 1, q, 0, behind).start()
             send(txt, 2 * NEAR, q, 2, partner).start()
 
         @pl.when(odd == 1)
         def _():
+            send(txt, 2 * FAR, q, 0, ahead).start()
             send(img, 2 * NEAR + 1, q, 2, partner).start()
 
         send(txt, 2 * GROUP, q, 3, lower).start()
+        return 0
+
+    def send_second(q, _):
+        @pl.when(odd == 0)
+        def _():
+            send(txt, 2 * FAR, q, 1, ahead).start()
+
+        @pl.when(odd == 1)
+        def _():
+            send(img, 2 * FAR + 1, q, 1, behind).start()
+
         send(img, 2 * GROUP + 1, q, 4, upper).start()
         return 0
 
-    lax.fori_loop(0, pieces, send_all, 0)
+    lax.fori_loop(0, pieces, send_first, 0)
+    lax.fori_loop(0, pieces, send_second, 0)
 
     for load in loads:
         load.wait()
@@ -129,11 +140,14 @@
         weight = jnp.where(s >= 0.0, 1.0, e) / (1.0 + e)
         if positive is not None:
             weight = weight - positive
-        if kind == 0:
+
+        @pl.when(kind == 0)
+        def _():
             loss = jnp.maximum(s, 0.0) + jnp.log1p(e)
             if positive is not None:
                 loss = loss - positive * s
             total[...] += loss
+
         w_high, w_low = split(scale * weight)
         w_both = jnp.concatenate([w_high, w_low], axis=1)
         for t in range(0, width, 384):
@@ -143,39 +157,65 @@
                 w_both, jnp.concatenate([top, top], axis=0), preferred_element_type=jnp.float32
             ) + jnp.dot(w_high, their_low[:, cut], preferred_element_type=jnp.float32)
 
-    def own_step(c, _):
+    def own_step(n, _):
+        c, kind = n // 2, n % 2
         at = pl.ds(pl.multiple_of(c * CHUNK, CHUNK), CHUNK)
-        for kind in range(2):
-            meet(kind, high[1 - kind, at], low[1 - kind, at], match[kind, c])
-        return 0
-
-    lax.fori_loop(0, chunks, own_step, 0)
-
-    def step(n, _):
-        c, m = n // 3, n % 3
+        meet(kind, high[1 - kind, at], low[1 - kind, at], match[kind, c])
+        return 0
+
+    lax.fori_loop(0, 2 * chunks, own_step, 0)
+
+    def visit(pair_of, kind, c):
+        slot = 2 * pair_of + kind
+        at = pl.ds(pl.multiple_of(c * CHUNK, CHUNK), CHUNK)
+        meet(kind, *split(land[slot, at]), None)
+
+    def early(n, _):
+        c, j = n // 4, n % 4
+        pair_of = (1 - (j + 2) // 3) * FAR + (j // 3) * NEAR
+        second = (j // 2) * (1 - j // 3)
+        kind = relayed + second * (odd - relayed)
         for h in range(PARTS):
             q = c * PARTS + h
-            arrived(2 * m + relayed, q)
-
-            @pl.when(m == FAR)
+            arrived(2 * pair_of + kind, q)
+
+            @pl.when(j == 0)
             def _():
                 relay(q).start()
 
+        visit(pair_of, kind, c)
+        return 0
+
+    lax.fori_loop(0, 4 * chunks, early, 0)
+
+    def store(kind, out):
+        return pltpu.make_async_copy(acc.at[kind], out, out_sem.at[kind])
+
+    @pl.when(odd == 0)
+    def _():
+        store(1, txt_out).start()
+
+    @pl.when(odd == 1)
+    def _():
+        store(0, img_out).start()
+
+    def late(n, _):
+        c, pair_of = n // 2, FAR + n % 2
         for h in range(PARTS):
-            arrived(2 * m + odd, c * PARTS + h)
-        at = pl.ds(pl.multiple_of(c * CHUNK, CHUNK), CHUNK)
-        for kind in range(2):
-            meet(kind, *split(land[2 * m + kind, at]), None)
-        return 0
-
-    lax.fori_loop(0, 3 * chunks, step, 0)
-
-    stores = [
-        pltpu.make_async_copy(acc.at[0], img_out, out_sem.at[0]),
-        pltpu.make_async_copy(acc.at[1], txt_out, out_sem.at[1]),
-    ]
-    for store in stores:
-        store.start()
+            arrived(2 * pair_of + odd, c * PARTS + h)
+        visit(pair_of, odd, c)
+        return 0
+
+    lax.fori_loop(0, 2 * chunks, late, 0)
+
+    @pl.when(odd == 0)
+    def _():
+        store(0, img_out).start()
+
+    @pl.when(odd == 1)
+    def _():
+        store(1, txt_out).start()
+
     loss_out[...] = jnp.sum(jnp.transpose(total[...]), axis=0, keepdims=True) / (4.0 * rows)
 
     def drain(q, _):
@@ -185,8 +225,8 @@
         return 0
 
     lax.fori_loop(0, pieces, drain, 0)
-    for store in stores:
-        store.wait()
+    store(0, img_out).wait()
+    store(1, txt_out).wait()
 
 
 def on_device(n_grp, n_blk, images, texts, pair_index):
@@ -216,7 +256,7 @@
             pltpu.SemaphoreType.DMA((6, pieces)),
         ],
         compiler_params=pltpu.CompilerParams(
-            collective_id=0, has_side_effects=True, vmem_limit_bytes=52 * 1024 * 1024
+            collective_id=0, has_side_effects=True, vmem_limit_bytes=60 * 1024 * 1024
         ),
         cost_estimate=pl.CostEstimate(
             flops=16 * 3 * 2 * rows * rows * width,

time: 105 us -> 96.1 us (0.915)
  Pallas kernels: 99.2 us -> 89.8 us
    pallas_call x1, Pallas kernels: 99.2 us -> 89.8 us  [on_device(): pl.pallas_call(functools.partial(kernel, n_grp, n_blk, scale), out_shape=...]
    unnamed x6 -> x4, local copies, waits for them, and re-layouts: 3.99 us -> 4.14 us
where the time goes in v1:
time: 96.1 us; the launch traced here: 95.9 us
  Pallas kernels  89.8 us (93%)
  local copies, waits for them, and re-layouts  4.14 us (4%)
  other arithmetic  1.28 us (1%)
    pallas_call x1, Pallas kernels, on_device(): pl.pallas_call(functools.partial(kernel, n_grp, n_blk, scale), out_shape=...  89.8 us
    unnamed x4, local copies, waits for them, and re-layouts  4.14 us

profile of v1, /device:TPU:0, one launch (start us, length us, event | category | flops | bytes accessed | tf_op | source)
XLA Modules:
  0.0 95.9 jit_solution(11946054864397598513)
XLA Ops:
  0.6 89.8 %shard_map.58 = (f32[1,384]{1,0:T(1,128)}, f32[384,1152]{1,0:T(8,128)}, f32[384,1152]{1,0:T(8,128)}) custom-call(f32[384,1152]{1,0:T(8,128)} %img.1, f32[384,1152]{1,0:T(8,128)} %txt.1, s32[1,384]{1,0:T(1,128)} %pair.1), custom_call_target="tpu_custom_call" | custom-call | flops 16307453952 | bytes 7077888 | tf_op jit(solution)/shard_map/pallas_call | solution.py:239
  90.5 1.3 %reduce = f32[384]{0:T(512)} reduce(f32[1,384]{1,0:T(1,128)} %get-tuple-element.6, f32[]{:T(128)} %constant.1), dimensions={0}, to_apply=%get-tuple-element.6.reduce_sub_computation | reduce | bytes 3076 | tf_op jit(solution)/shard_map/pallas_call | solution.py:239
  91.8 0.0 copy-start
  91.8 2.9 %copy.8 = f32[384,1152]{1,0:T(8,128)} copy(f32[384,1152]{1,0:T(8,128)} %get-tuple-element.13) | data formatting | bytes 3538944
  94.7 0.0 copy-done
  94.7 1.2 %copy.9 = f32[384,1152]{1,0:T(8,128)} copy(f32[384,1152]{1,0:T(8,128)S(1)} %copy-done) | data formatting | bytes 3538944
Async XLA Ops:
  91.8 2.9 %copy-start = (f32[384,1152]{1,0:T(8,128)S(1)}, f32[384,1152]{1,0:T(8,128)}, u32[]{:S(2)}) copy-start(f32[384,1152]{1,0:T(8,128)} %get-tuple-element.14) | copy-start | bytes 5308420

commit v2 on v1

--- a/solution.py
+++ b/solution.py
@@ -11,6 +11,7 @@
 CHUNK = 128
 PIECE = 64
 PARTS = CHUNK // PIECE
+STRIPS = 2
 
 GROUP, FAR, NEAR = 0, 1, 2
 
@@ -26,8 +27,8 @@
 
 def kernel(
     n_grp, n_blk, scale,
-    img, txt, pair, loss_out, img_out, txt_out,
-    land, own, high, low, acc, match, total,
+    img, txt, pair_in, loss_out, img_out, txt_out,
+    pair, loss_row, land, own, high, low, acc, match, total,
     own_sem, out_sem, send_sem, relay_sem, recv_sem,
 ):
     rows, width = img.shape
@@ -43,6 +44,7 @@
     loads = [
         pltpu.make_async_copy(img, own.at[0], own_sem.at[0]),
         pltpu.make_async_copy(txt, own.at[1], own_sem.at[1]),
+        pltpu.make_async_copy(pair_in, pair, own_sem.at[2]),
     ]
     for load in loads:
         load.start()
@@ -216,7 +218,9 @@
     def _():
         store(1, txt_out).start()
 
-    loss_out[...] = jnp.sum(jnp.transpose(total[...]), axis=0, keepdims=True) / (4.0 * rows)
+    loss_row[...] = jnp.sum(jnp.transpose(total[...]), axis=0, keepdims=True) / (4.0 * rows)
+    store_loss = pltpu.make_async_copy(loss_row, loss_out, out_sem.at[2])
+    store_loss.start()
 
     def drain(q, _):
         for line, device in enumerate((ahead, behind, partner, lower, upper)):
@@ -227,6 +231,45 @@
     lax.fori_loop(0, pieces, drain, 0)
     store(0, img_out).wait()
     store(1, txt_out).wait()
+    store_loss.wait()
+
+
+def finish(
+    loss, img_part, txt_part, loss_out, img_out, txt_out, row, line, held, in_sem, out_sem
+):
+    rows = img_part.shape[0]
+    step = rows // STRIPS
+
+    def part(n):
+        return pl.ds(n * step, step)
+
+    def load(kind, n):
+        source = (img_part, txt_part)[kind]
+        return pltpu.make_async_copy(
+            source.at[part(n)], held.at[kind, part(n)], in_sem.at[1 + kind * STRIPS + n]
+        )
+
+    def store(kind, n):
+        target = (img_out, txt_out)[kind]
+        return pltpu.make_async_copy(
+            held.at[kind, part(n)], target.at[part(n)], out_sem.at[1 + kind * STRIPS + n]
+        )
+
+    order = [(kind, n) for n in range(STRIPS) for kind in range(2)]
+    load_loss = pltpu.make_async_copy(loss, row, in_sem.at[0])
+    store_loss = pltpu.make_async_copy(line, loss_out, out_sem.at[0])
+    load_loss.start()
+    for item in order:
+        load(*item).start()
+    load_loss.wait()
+    line[...] = row[0]
+    store_loss.start()
+    for item in order:
+        load(*item).wait()
+        store(*item).start()
+    for item in order:
+        store(*item).wait()
+    store_loss.wait()
 
 
 def on_device(n_grp, n_blk, images, texts, pair_index):
@@ -234,14 +277,16 @@
     scale = 2.0 * width ** (-0.5)
     pieces = rows // PIECE
     any_space = pl.BlockSpec(memory_space=pl.ANY)
-    vmem = pl.BlockSpec(memory_space=pltpu.VMEM)
+    limit = 60 * 1024 * 1024
     block = jax.ShapeDtypeStruct((rows, width), jnp.float32)
     loss, image_grad, text_grad = pl.pallas_call(
         functools.partial(kernel, n_grp, n_blk, scale),
         out_shape=(jax.ShapeDtypeStruct((1, rows), jnp.float32), block, block),
-        in_specs=[any_space, any_space, vmem],
-        out_specs=(vmem, any_space, any_space),
+        in_specs=[any_space] * 3,
+        out_specs=(any_space,) * 3,
         scratch_shapes=[
+            pltpu.VMEM((1, rows), jnp.int32),
+            pltpu.VMEM((1, rows), jnp.float32),
             pltpu.VMEM((6, rows, width), jnp.float32),
             pltpu.VMEM((2, rows, width), jnp.float32),
             pltpu.VMEM((2, rows, width), jnp.bfloat16),
@@ -249,14 +294,14 @@
             pltpu.VMEM((2, rows, width), jnp.float32),
             pltpu.VMEM((2, rows // CHUNK, rows, CHUNK), jnp.float32),
             pltpu.VMEM((rows, CHUNK), jnp.float32),
-            pltpu.SemaphoreType.DMA((2,)),
-            pltpu.SemaphoreType.DMA((2,)),
+            pltpu.SemaphoreType.DMA((3,)),
+            pltpu.SemaphoreType.DMA((3,)),
             pltpu.SemaphoreType.DMA((5, pieces)),
             pltpu.SemaphoreType.DMA((pieces,)),
             pltpu.SemaphoreType.DMA((6, pieces)),
         ],
         compiler_params=pltpu.CompilerParams(
-            collective_id=0, has_side_effects=True, vmem_limit_bytes=60 * 1024 * 1024
+            collective_id=0, has_side_effects=True, vmem_limit_bytes=limit
         ),
         cost_estimate=pl.CostEstimate(
             flops=16 * 3 * 2 * rows * rows * width,
@@ -264,7 +309,23 @@
             transcendentals=8 * rows * rows,
         ),
     )(images, texts, pair_index)
-    return loss.reshape(rows), image_grad, text_grad
+    return pl.pallas_call(
+        finish,
+        out_shape=(jax.ShapeDtypeStruct((rows,), jnp.float32), block, block),
+        in_specs=[any_space] * 3,
+        out_specs=(any_space,) * 3,
+        scratch_shapes=[
+            pltpu.VMEM((1, rows), jnp.float32),
+            pltpu.VMEM((rows,), jnp.float32),
+            pltpu.VMEM((2, rows, width), jnp.float32),
+            pltpu.SemaphoreType.DMA((1 + 2 * STRIPS,)),
+            pltpu.SemaphoreType.DMA((1 + 2 * STRIPS,)),
+        ],
+        compiler_params=pltpu.CompilerParams(vmem_limit_bytes=limit),
+        cost_estimate=pl.CostEstimate(
+            flops=0, bytes_accessed=4 * 4 * rows * width, transcendentals=0
+        ),
+    )(loss, image_grad, text_grad)
 
 
 def solution(mesh):

time: 96.1 us -> 92.5 us (0.963)
  local copies, waits for them, and re-layouts: 4.14 us -> 0 us
  Pallas kernels: 89.8 us -> 91.7 us
  other arithmetic: 1.28 us -> 0 us
    unnamed x4 -> x0, local copies, waits for them, and re-layouts: 4.14 us -> none
    pallas_call x0 -> x1, Pallas kernels: none -> 3.04 us  [on_device(): pl.pallas_call(finish, out_shape=(jax.ShapeDtypeStruct((rows,), jnp.float...]
    pallas_call x1 -> x0, other arithmetic: 1.28 us -> none  [on_device(): pl.pallas_call(functools.partial(kernel, n_grp, n_blk, scale), out_shape=...]
    pallas_call x1, Pallas kernels: 89.8 us -> 88.7 us  [on_device(): pl.pallas_call(functools.partial(kernel, n_grp, n_blk, scale), out_shape=...]
where the time goes in v2:
time: 92.5 us; the launch traced here: 92.3 us
  Pallas kernels  91.7 us (99%)
    pallas_call x1, Pallas kernels, on_device(): pl.pallas_call(functools.partial(kernel, n_grp, n_blk, scale), out_shape=...  88.7 us
    pallas_call x1, Pallas kernels, on_device(): pl.pallas_call(finish, out_shape=(jax.ShapeDtypeStruct((rows,), jnp.float...  3.04 us

profile of v2, /device:TPU:0, one launch (start us, length us, event | category | flops | bytes accessed | tf_op | source)
XLA Modules:
  0.0 92.3 jit_solution(6620723097344632880)
XLA Ops:
  0.6 88.7 %shard_map.58 = (f32[1,384]{1,0:T(1,128)}, f32[384,1152]{1,0:T(8,128)}, f32[384,1152]{1,0:T(8,128)}) custom-call(f32[384,1152]{1,0:T(8,128)} %img.1, f32[384,1152]{1,0:T(8,128)} %txt.1, s32[1,384]{1,0:T(1,128)} %pair_in.1), custom_call_target="tpu_custom_call" | custom-call | flops 16307453952 | bytes 7077888 | tf_op jit(solution)/shard_map/pallas_call | solution.py:282
  89.3 3.0 %shard_map.59 = (f32[384]{0:T(512)}, f32[384,1152]{1,0:T(8,128)}, f32[384,1152]{1,0:T(8,128)}) custom-call(f32[1,384]{1,0:T(1,128)} %get-tuple-element.6.loss, f32[384,1152]{1,0:T(8,128)} %get-tuple-element.7.img_part, f32[384,1152]{1,0:T(8,128)} %get-tuple-element.8.txt_part), custom_call_target="tpu_custom_call" | custom-call | bytes 7077888 | tf_op jit(solution)/shard_map/pallas_call | solution.py:312

commit v3 on v2

--- a/solution.py
+++ b/solution.py
@@ -11,6 +11,7 @@
 CHUNK = 128
 PIECE = 64
 PARTS = CHUNK // PIECE
+HALF = CHUNK // 2
 STRIPS = 2
 
 GROUP, FAR, NEAR = 0, 1, 2
@@ -202,10 +203,14 @@
         store(0, img_out).start()
 
     def late(n, _):
-        c, pair_of = n // 2, FAR + n % 2
-        for h in range(PARTS):
-            arrived(2 * pair_of + odd, c * PARTS + h)
-        visit(pair_of, odd, c)
+        for h in range(PARTS // 2):
+            arrived(2 * FAR + odd, n * (PARTS // 2) + h)
+            arrived(2 * NEAR + odd, n * (PARTS // 2) + h)
+        at = pl.ds(pl.multiple_of(n * HALF, HALF), HALF)
+        theirs = jnp.concatenate(
+            [land[2 * FAR + odd, at], land[2 * NEAR + odd, at]], axis=0
+        )
+        meet(odd, *split(theirs), None)
         return 0
 
     lax.fori_loop(0, 2 * chunks, late, 0)

time: 92.5 us -> 91 us (0.984)
  Pallas kernels: 91.7 us -> 90.2 us
    pallas_call x1, Pallas kernels: 88.7 us -> 87.1 us  [on_device(): pl.pallas_call(functools.partial(kernel, n_grp, n_blk, scale), out_shape=...]
where the time goes in v3:
time: 91 us; the launch traced here: 90.8 us
  Pallas kernels  90.2 us (99%)
    pallas_call x1, Pallas kernels, on_device(): pl.pallas_call(functools.partial(kernel, n_grp, n_blk, scale), out_shape=...  87.1 us
    pallas_call x1, Pallas kernels, on_device(): pl.pallas_call(finish, out_shape=(jax.ShapeDtypeStruct((rows,), jnp.float...  3.04 us

profile of v3, /device:TPU:0, one launch (start us, length us, event | category | flops | bytes accessed | tf_op | source)
XLA Modules:
  0.0 90.8 jit_solution(7247022590833411893)
XLA Ops:
  0.6 87.1 %shard_map.58 = (f32[1,384]{1,0:T(1,128)}, f32[384,1152]{1,0:T(8,128)}, f32[384,1152]{1,0:T(8,128)}) custom-call(f32[384,1152]{1,0:T(8,128)} %img.1, f32[384,1152]{1,0:T(8,128)} %txt.1, s32[1,384]{1,0:T(1,128)} %pair_in.1), custom_call_target="tpu_custom_call" | custom-call | flops 16307453952 | bytes 7077888 | tf_op jit(solution)/shard_map/pallas_call | solution.py:287
  87.8 3.0 %shard_map.59 = (f32[384]{0:T(512)}, f32[384,1152]{1,0:T(8,128)}, f32[384,1152]{1,0:T(8,128)}) custom-call(f32[1,384]{1,0:T(1,128)} %get-tuple-element.6.loss, f32[384,1152]{1,0:T(8,128)} %get-tuple-element.7.img_part, f32[384,1152]{1,0:T(8,128)} %get-tuple-element.8.txt_part), custom_call_target="tpu_custom_call" | custom-call | bytes 7077888 | tf_op jit(solution)/shard_map/pallas_call | solution.py:317

commit v4 on v3

--- a/solution.py
+++ b/solution.py
@@ -135,7 +135,7 @@
     acc[...] = jnp.zeros_like(acc)
     total[...] = jnp.zeros_like(total)
 
-    def meet(kind, their_high, their_low, positive):
+    def meet(kind, their_high, their_low, positive, leave=None):
         both = across(high[kind], jnp.concatenate([their_high, their_low], axis=0))
         dots = both[:, :CHUNK] + both[:, CHUNK:] + across(low[kind], their_high)
         s = scale * dots - 3.0
@@ -159,6 +159,8 @@
             acc[kind, :, cut] += jnp.dot(
                 w_both, jnp.concatenate([top, top], axis=0), preferred_element_type=jnp.float32
             ) + jnp.dot(w_high, their_low[:, cut], preferred_element_type=jnp.float32)
+            if leave is not None:
+                leave(cut)
 
     def own_step(n, _):
         c, kind = n // 2, n % 2
@@ -202,7 +204,19 @@
     def _():
         store(0, img_out).start()
 
-    def late(n, _):
+    def leave(cut):
+        def strip(kind, out):
+            return pltpu.make_async_copy(acc.at[kind, :, cut], out.at[:, cut], out_sem.at[kind])
+
+        @pl.when(odd == 0)
+        def _():
+            strip(0, img_out).start()
+
+        @pl.when(odd == 1)
+        def _():
+            strip(1, txt_out).start()
+
+    def late(n, leave=None):
         for h in range(PARTS // 2):
             arrived(2 * FAR + odd, n * (PARTS // 2) + h)
             arrived(2 * NEAR + odd, n * (PARTS // 2) + h)
@@ -210,18 +224,13 @@
         theirs = jnp.concatenate(
             [land[2 * FAR + odd, at], land[2 * NEAR + odd, at]], axis=0
         )
-        meet(odd, *split(theirs), None)
-        return 0
-
-    lax.fori_loop(0, 2 * chunks, late, 0)
-
-    @pl.when(odd == 0)
-    def _():
-        store(0, img_out).start()
-
-    @pl.when(odd == 1)
-    def _():
-        store(1, txt_out).start()
+        meet(odd, *split(theirs), None, leave)
+
+    @pl.loop(0, 2 * chunks - 1)
+    def _(n):
+        late(n)
+
+    late(2 * chunks - 1, leave)
 
     loss_row[...] = jnp.sum(jnp.transpose(total[...]), axis=0, keepdims=True) / (4.0 * rows)
     store_loss = pltpu.make_async_copy(loss_row, loss_out, out_sem.at[2])

time: 91 us -> 90.6 us (level)
  no operation moved by 1% of the time
where the time goes in v4:
time: 90.6 us; the launch traced here: 90.5 us
  Pallas kernels  89.9 us (99%)
    pallas_call x1, Pallas kernels, on_device(): pl.pallas_call(functools.partial(kernel, n_grp, n_blk, scale), out_shape=...  86.8 us
    pallas_call x1, Pallas kernels, on_device(): pl.pallas_call(finish, out_shape=(jax.ShapeDtypeStruct((rows,), jnp.float...  3.04 us

profile of v4, /device:TPU:0, one launch (start us, length us, event | category | flops | bytes accessed | tf_op | source)
XLA Modules:
  0.0 90.5 jit_solution(11934474748667486437)
XLA Ops:
  0.6 86.8 %shard_map.58 = (f32[1,384]{1,0:T(1,128)}, f32[384,1152]{1,0:T(8,128)}, f32[384,1152]{1,0:T(8,128)}) custom-call(f32[384,1152]{1,0:T(8,128)} %img.1, f32[384,1152]{1,0:T(8,128)} %txt.1, s32[1,384]{1,0:T(1,128)} %pair_in.1), custom_call_target="tpu_custom_call" | custom-call | flops 16307453952 | bytes 7077888 | tf_op jit(solution)/shard_map/pallas_call | solution.py:296
  87.4 3.0 %shard_map.59 = (f32[384]{0:T(512)}, f32[384,1152]{1,0:T(8,128)}, f32[384,1152]{1,0:T(8,128)}) custom-call(f32[1,384]{1,0:T(1,128)} %get-tuple-element.6.loss, f32[384,1152]{1,0:T(8,128)} %get-tuple-element.7.img_part, f32[384,1152]{1,0:T(8,128)} %get-tuple-element.8.txt_part), custom_call_target="tpu_custom_call" | custom-call | bytes 7077888 | tf_op jit(solution)/shard_map/pallas_call | solution.py:326
